TPU v7x, 512 devices: a whole 4x8x8 slice. The times are simulated.
512 devices in a mesh: cuts: 4 (over x), tile: 128 (over y, z, core).
Axes of the slice: x: 4, y: 8, z: 8, core: 2. Of those that a mesh axis runs over, the one named last changes fastest.
Arguments:
- object_field: float32 [4, 2, 32768, 1024], P('cuts', None, 'tile'), may hold values from -6 to 6
- probe_wave: bfloat16 [2, 256, 256], replicated, may hold values from -6 to 6
- chirp_phase: float32 [256], replicated, may hold values from -3.140625 to 3.140625
- amplitude: bfloat16 [256, 256, 256], P('tile'), may hold values from 0 to 2
- scan_row: int32 [256], P('tile'), may hold values from 0 to 255
- scan_col: int32 [256], P('tile'), may hold values from 0 to 768
- view_count: int32 [128], P('tile'), may hold values from 1 to 2, 192 in all
Outputs:
- object_grad: float32 [4, 2, 32768, 1024], P('cuts', None, 'tile')
All inputs are finite; a program needn't handle non-finite values. No bound on the sum of `view_count` on one device may be relied on, other than what follows from the above.
Results may differ from a plain program's by a relative error of at most 0.04.
Values may be sent and summed in bfloat16 or wider, within the bound.
A program may use at most 64 MiB of HBM per device.

v0:
```python
import math

import jax
import jax.numpy as jnp
from jax import lax
from jax.sharding import PartitionSpec as P


def shifted(shard, axis, by):
    size = lax.axis_size(axis)
    return lax.ppermute(shard, axis, [(i, (i + by) % size) for i in range(size)])


def shifted_2(value, axis, steps):
    count = lax.axis_size(axis)
    first, last = (max(0, -steps), min(count, count - steps))
    return lax.ppermute(value, axis, [(source, source + steps) for source in range(first, last)])


def block_matrix(real_part, imag_part):
    upper_half = jnp.stack([real_part, -imag_part], axis=1)
    lower_half = jnp.stack([imag_part, real_part], axis=1)
    return jnp.stack([upper_half, lower_half], axis=0).astype(jnp.bfloat16)


def operator_tables(chirp_phase):
    length = chirp_phase.shape[0]
    indices = jnp.arange(length, dtype=jnp.int32)
    product = indices[:, None] * indices[None, :] % length
    phase_angle = product.astype(jnp.float32) * jnp.float32(2.0 * math.pi / length)
    fourier_real = jnp.cos(phase_angle)
    fourier_imag = -jnp.sin(phase_angle)
    cosine = jnp.cos(chirp_phase)[:, None]
    sine = jnp.sin(chirp_phase)[:, None]
    scaled_real = cosine * fourier_real - sine * fourier_imag
    scaled_imag = cosine * fourier_imag + sine * fourier_real
    highest = lax.Precision.HIGHEST
    prop_real = (
        jnp.dot(fourier_real, scaled_real, precision=highest)
        + jnp.dot(fourier_imag, scaled_imag, precision=highest)
    ) / length
    prop_imag = (
        jnp.dot(fourier_real, scaled_imag, precision=highest)
        - jnp.dot(fourier_imag, scaled_real, precision=highest)
    ) / length
    root = math.sqrt(length)
    return (
        block_matrix(prop_real, prop_imag),
        block_matrix(fourier_real / root, fourier_imag / root),
    )


def apply_left(matrix, wavefield):
    return jnp.einsum("dicj,vcjx->vdix", matrix, wavefield, preferred_element_type=jnp.float32)


def apply_right(matrix, wavefield):
    return jnp.einsum("vcyj,dicj->vdyi", wavefield, matrix, preferred_element_type=jnp.float32)


def back_left(matrix, gradient):
    return jnp.einsum("dicj,vdix->vcjx", matrix, gradient, preferred_element_type=jnp.float32)


def back_right(matrix, gradient):
    return jnp.einsum("vdyi,dicj->vcyj", gradient, matrix, preferred_element_type=jnp.float32)


def transform(matrix, wavefield):
    half_done = apply_left(matrix, wavefield).astype(jnp.bfloat16)
    return apply_right(matrix, half_done)


def transform_back(matrix, gradient):
    half_done = back_right(matrix, gradient.astype(jnp.bfloat16)).astype(jnp.bfloat16)
    return back_left(matrix, half_done)


def through_slice(matrix, wavefield, window_batch):
    wave_real = wavefield[:, 0]
    wave_imag = wavefield[:, 1]
    product = jnp.stack(
        [
            wave_real * window_batch[:, 0] - wave_imag * window_batch[:, 1],
            wave_real * window_batch[:, 1] + wave_imag * window_batch[:, 0],
        ],
        axis=1,
    )
    return transform(matrix, product.astype(jnp.bfloat16))


def slice_back(matrix, gradient, wavefield, window_batch):
    grad_product = transform_back(matrix, gradient)
    grad_real = grad_product[:, 0]
    grad_imag = grad_product[:, 1]
    wave_real = wavefield[:, 0]
    wave_imag = wavefield[:, 1]
    grad_object = jnp.stack(
        [
            grad_real * wave_real + grad_imag * wave_imag,
            grad_imag * wave_real - grad_real * wave_imag,
        ],
        axis=1,
    )
    grad_wave = jnp.stack(
        [
            grad_real * window_batch[:, 0] + grad_imag * window_batch[:, 1],
            grad_imag * window_batch[:, 0] - grad_real * window_batch[:, 1],
        ],
        axis=1,
    )
    return (grad_object, grad_wave)


def far_residual(matrix, exit_wave, amplitude, live_slots):
    far_field = transform(matrix, exit_wave.astype(jnp.bfloat16))
    modulus = jnp.sqrt(far_field[:, 0] * far_field[:, 0] + far_field[:, 1] * far_field[:, 1] + 0.01)
    factor = live_slots[:, None, None] * (modulus - amplitude.astype(jnp.float32)) / modulus
    gradient = (far_field * factor[:, None]).astype(jnp.bfloat16)
    return transform_back(matrix, gradient)


def cut_windows(frame, start_rows, start_cols, side_length):
    layers = frame.shape[0]
    pieces = []
    for view_index in range(start_rows.shape[0]):
        pieces.append(
            lax.dynamic_slice(
                frame,
                (0, 0, start_rows[view_index], start_cols[view_index]),
                (layers, 2, side_length, side_length),
            )
        )
    return jnp.stack(pieces, axis=1)


def scatter_windows(frame, gradients, start_rows, start_cols):
    layers = frame.shape[0]
    side_length = gradients.shape[-1]
    for view_index in range(start_rows.shape[0]):
        corner = (0, 0, start_rows[view_index], start_cols[view_index])
        current = lax.dynamic_slice(frame, corner, (layers, 2, side_length, side_length))
        frame = lax.dynamic_update_slice(frame, current + gradients[:, view_index], corner)
    return frame


def body(object_field, probe_wave, chirp_phase, amplitude, scan_row, scan_col, view_count):
    propagator, far_matrix = operator_tables(chirp_phase)
    layers = object_field.shape[0]
    tile_rows = object_field.shape[2]
    side_length = probe_wave.shape[-1]
    view_slots = scan_row.shape[0]
    position = lax.axis_index("cuts")
    sections = lax.axis_size("cuts")
    live_slots = (jnp.arange(view_slots, dtype=jnp.int32) < view_count[0]).astype(jnp.float32)
    following = shifted(object_field, "tile", -1)
    extended = jnp.concatenate([object_field, following], axis=2)
    all_windows = cut_windows(extended, scan_row, scan_col, side_length)
    windows = [all_windows[0]]
    wave_shape = (view_slots, 2, side_length, side_length)
    probe_float = probe_wave.astype(jnp.float32)
    saved = [jnp.zeros(wave_shape, jnp.float32)]
    grads = [jnp.zeros(wave_shape, jnp.float32)]
    incoming = jnp.broadcast_to(probe_float[None], wave_shape)
    wavefield = incoming
    for section_index in range(sections):
        is_mine = position == section_index
        wavefield = incoming
        layer_index = 0
        saved[layer_index] = jnp.where(is_mine, wavefield, saved[layer_index])
        wavefield = through_slice(propagator, wavefield, windows[layer_index])
        if section_index < sections - 1:
            incoming = shifted_2(wavefield, "cuts", 1)
    cotangent = far_residual(far_matrix, wavefield, amplitude, live_slots)
    for section_index in reversed(range(sections)):
        is_mine = position == section_index
        grad_wave = cotangent
        for layer_index in reversed(range(layers)):
            grad_object, grad_wave = slice_back(
                propagator, grad_wave, saved[layer_index], windows[layer_index]
            )
            grads[layer_index] = jnp.where(is_mine, grad_object, grads[layer_index])
        if section_index > 0:
            cotangent = shifted_2(grad_wave.astype(jnp.bfloat16), "cuts", -1)
    grad_windows = jnp.stack(grads, axis=0)
    frame_shape = (layers, 2, 2 * tile_rows, object_field.shape[3])
    frame_total = scatter_windows(
        jnp.zeros(frame_shape, jnp.float32), grad_windows, scan_row, scan_col
    )
    spilled = shifted(frame_total[:, :, tile_rows:], "tile", 1)
    return frame_total[:, :, :tile_rows] + spilled


def solution(mesh):
    in_specs = (
        P("cuts", None, "tile", None),
        P(),
        P(),
        P("tile", None, None),
        P("tile"),
        P("tile"),
        P("tile"),
    )
    out_specs = P("cuts", None, "tile", None)
    return jax.shard_map(body, mesh=mesh, in_specs=in_specs, out_specs=out_specs, check_vma=False)
```

profile of v0, /device:TPU:2, one launch (start us, length us, event | category | flops | bytes accessed | tf_op | source)
XLA Modules:
  0.0 236.6 jit_solution(9504413862971824939)
XLA Ops:
  0.0 13.3 %collective-permute-start = (f32[1,2,256,1024]{3,2,1,0:T(8,128)}, f32[1,2,256,1024]{3,2,1,0:T(8,128)S(1)}, u32[]{:S(2)}, u32[]{:S(2)}) collective-permute-start(f32[1,2,256,1024]{3,2,1,0:T(8,128)} %param.7), channel_id=1, source_target_pairs={{0,127},{1,0},{2,1},{3,2},{4,3},{5,4},{6,5},{7,6},{8,7},{9,8},{10,... | collective-permute-start | bytes 6291464 | tf_op jit(solution)/shard_map/ppermute | solution.py:11
  13.3 1.3 fusion.129
  17.1 1.3 fusion.128
  20.9 1.0 convert_element_type.139
  24.7 0.7 fusion.127
  25.4 1.5 fusion.82
  26.9 1.5 fusion.19
  28.4 1.5 fusion.81
  29.8 1.5 fusion.88
  31.4 0.2 constant_dynamic-update-slice_fusion.1
  31.6 5.5 %collective-permute-done = f32[1,2,256,1024]{3,2,1,0:T(8,128)S(1)} collective-permute-done((f32[1,2,256,1024]{3,2,1,0:T(8,128)}, f32[1,2,256,1024]{3,2,1,0:T(8,128)S(1)}, u32[]{:S(2)}, u32[]{:S(2)}) %collective-permute-start) | collective-permute-done | bytes 2097184 | tf_op jit(solution)/shard_map/ppermute | solution.py:11
  37.1 0.2 constant_dynamic-update-slice_fusion
  37.4 0.4 constant_dynamic-slice_fusion.1
  38.4 1.8 convolution_bitcast_fusion.14
  40.2 3.4 %collective-permute-start.1 = (f32[2,2,256,256]{2,3,0,1:T(8,128)}, f32[2,2,256,256]{2,3,0,1:T(8,128)S(1)}, u32[]{:S(2)}, u32[]{:S(2)}) collective-permute-start(f32[2,2,256,256]{2,3,0,1:T(8,128)} %convolution_bitcast_fusion.14), channel_id=1, source_target_pairs={{0,128},{128,256},{256,384},{1,129},{129,257},{257,385},{2,130},{1... | collective-permute-start | bytes 3145736 | tf_op jit(solution)/shard_map/ppermute | solution.py:17
  43.6 16.9 %collective-permute-done.1 = f32[2,2,256,256]{2,3,0,1:T(8,128)S(1)} collective-permute-done((f32[2,2,256,256]{2,3,0,1:T(8,128)}, f32[2,2,256,256]{2,3,0,1:T(8,128)S(1)}, u32[]{:S(2)}, u32[]{:S(2)}) %collective-permute-start.1) | collective-permute-done | bytes 1048608 | tf_op jit(solution)/shard_map/ppermute | solution.py:17
  60.4 1.0 copy-done.2
  61.6 1.8 convolution_bitcast_fusion.12
  63.4 3.5 %collective-permute-start.2 = (f32[2,2,256,256]{2,3,0,1:T(8,128)}, f32[2,2,256,256]{2,3,0,1:T(8,128)S(1)}, u32[]{:S(2)}, u32[]{:S(2)}) collective-permute-start(f32[2,2,256,256]{2,3,0,1:T(8,128)} %convolution_bitcast_fusion.12), channel_id=1, source_target_pairs={{0,128},{128,256},{256,384},{1,129},{129,257},{257,385},{2,130},{1... | collective-permute-start | bytes 3145736 | tf_op jit(solution)/shard_map/ppermute | solution.py:17
  66.9 17.0 %collective-permute-done.2 = f32[2,2,256,256]{2,3,0,1:T(8,128)S(1)} collective-permute-done((f32[2,2,256,256]{2,3,0,1:T(8,128)}, f32[2,2,256,256]{2,3,0,1:T(8,128)S(1)}, u32[]{:S(2)}, u32[]{:S(2)}) %collective-permute-start.2) | collective-permute-done | bytes 1048608 | tf_op jit(solution)/shard_map/ppermute | solution.py:17
  83.9 1.0 copy-done.4
  85.0 1.8 convolution_bitcast_fusion.10
  86.8 3.6 %collective-permute-start.3 = (f32[2,2,256,256]{2,3,0,1:T(8,128)}, f32[2,2,256,256]{2,3,0,1:T(8,128)S(1)}, u32[]{:S(2)}, u32[]{:S(2)}) collective-permute-start(f32[2,2,256,256]{2,3,0,1:T(8,128)} %convolution_bitcast_fusion.10), channel_id=1, source_target_pairs={{0,128},{128,256},{256,384},{1,129},{129,257},{257,385},{2,130},{1... | collective-permute-start | bytes 3145736 | tf_op jit(solution)/shard_map/ppermute | solution.py:17
  91.2 1.0 fusion.87
  92.2 1.1 negate_convert_fusion
  93.4 0.9 maximum_bitcast_fusion.7
  94.3 9.4 %collective-permute-done.3 = f32[2,2,256,256]{2,3,0,1:T(8,128)S(1)} collective-permute-done((f32[2,2,256,256]{2,3,0,1:T(8,128)}, f32[2,2,256,256]{2,3,0,1:T(8,128)S(1)}, u32[]{:S(2)}, u32[]{:S(2)}) %collective-permute-start.3) | collective-permute-done | bytes 1048608 | tf_op jit(solution)/shard_map/ppermute | solution.py:17
  103.9 0.5 convolution_convert_fusion.3
  104.4 0.5 copy.141
  104.9 0.4 convolution_convert_fusion.2
  105.4 0.5 copy.140
  105.9 2.0 convolution_bitcast_fusion.8
  107.9 0.3 multiply_divide_fusion
  108.2 1.5 convolution_convert_fusion.1
  109.8 0.5 copy.139
  110.3 0.4 convolution_convert_fusion
  110.8 0.5 copy.138
  111.3 0.8 convolution_bitcast_fusion.7
  112.3 1.9 collective-permute-start.4
  114.3 14.2 %collective-permute-done.4 = bf16[2,2,256,256]{2,3,0,1:T(8,128)(2,1)} collective-permute-done((bf16[2,2,256,256]{2,3,0,1:T(8,128)(2,1)S(1)}, bf16[2,2,256,256]{2,3,0,1:T(8,128)(2,1)}, u32[]{:S(2)}, u32[]{:S(2)}) %collective-permute-start.4) | collective-permute-done | bytes 524320 | tf_op jit(solution)/shard_map/ppermute | solution.py:17
  128.4 2.1 convolution_bitcast_fusion.6
  130.7 0.8 pad_maximum_fusion.3
  131.6 1.9 collective-permute-start.5
  133.5 0.9 broadcast_select_fusion
  134.4 2.0 copy.21
  136.4 11.3 %collective-permute-done.5 = bf16[2,2,256,256]{2,3,0,1:T(8,128)(2,1)} collective-permute-done((bf16[2,2,256,256]{2,3,0,1:T(8,128)(2,1)}, bf16[2,2,256,256]{2,3,0,1:T(8,128)(2,1)}, u32[]{:S(2)}, u32[]{:S(2)}) %collective-permute-start.5) | collective-permute-done | bytes 524320 | tf_op jit(solution)/shard_map/ppermute | solution.py:17
  147.7 3.1 %convolution_bitcast_fusion.5 = f32[2,2,256,256]{2,3,0,1:T(8,128)} fusion(bf16[2,256,2,256,1]{3,1,2,0,4:T(8,128)(2,1)} %copy-done.13, bf16[2,2,256,256]{2,3,0,1:T(8,128)(2,1)} %collective-permute-done.5), kind=kOutput, calls=%fused_computation.6 | convolution fusion | flops 537133056 | bytes 2097152 | tf_op jit(solution)/shard_map/dicj,vdix->vcjx/dot_general | solution.py:62
  150.8 1.5 add_convert_fusion
  152.4 2.1 collective-permute-start.6
  154.6 1.4 select_select_fusion
  156.0 1.6 add_bitcast_fusion
  157.6 6.0 %collective-permute-done.6 = bf16[2,2,256,256]{2,3,0,1:T(8,128)(2,1)} collective-permute-done((bf16[2,2,256,256]{2,3,0,1:T(8,128)(2,1)S(1)}, bf16[2,2,256,256]{2,3,0,1:T(8,128)(2,1)}, u32[]{:S(2)}, u32[]{:S(2)}) %collective-permute-start.6) | collective-permute-done | bytes 524320 | tf_op jit(solution)/shard_map/ppermute | solution.py:17
  163.6 3.1 %convolution_bitcast_fusion.4 = f32[2,2,256,256]{2,3,0,1:T(8,128)} fusion(bf16[2,256,2,256,1]{3,1,2,0,4:T(8,128)(2,1)} %copy-done.13, bf16[2,2,256,256]{2,3,0,1:T(8,128)(2,1)} %collective-permute-done.6), kind=kOutput, calls=%fused_computation.5 | convolution fusion | flops 537133056 | bytes 2097152 | tf_op jit(solution)/shard_map/dicj,vdix->vcjx/dot_general | solution.py:62
  166.7 1.5 add_bitcast_fusion.1
  168.3 0.4 maximum_select_fusion
  168.7 2.5 %broadcast_in_dim.8 = f32[1,2,512,1024]{2,3,1,0:T(8,128)} broadcast(f32[]{:T(128)} %constant.16.clone.1), dimensions={} | broadcast | bytes 4194308 | tf_op jit(solution)/shard_map/broadcast_in_dim | solution.py:188
  171.2 6.8 %dynamic_update_slice.6 = f32[1,2,512,1024]{2,3,1,0:T(8,128)} dynamic-update-slice(f32[1,2,512,1024]{2,3,1,0:T(8,128)} %broadcast_in_dim.8, f32[1,2,256,256]{2,3,1,0:T(8,128)S(1)} %slice_bitcast_fusion.1, s32[]{:T(128)} %constant.37.clone.1, s32[]{:T(128)} %constant.37.clone.1, s32[]{:T(128)S(6)} %select_n.144, s32[]{:T(128)S(6)} %select_n.145) | dynamic-update-slice | bytes 1048580 | tf_op jit(solution)/shard_map/dynamic_update_slice | solution.py:143
  178.0 1.4 fusion.21
  179.4 6.5 %dynamic_update_slice.7 = f32[1,2,512,1024]{2,3,1,0:T(8,128)} dynamic-update-slice(f32[1,2,512,1024]{2,3,1,0:T(8,128)} %dynamic_update_slice.6, f32[1,2,256,256]{2,3,1,0:T(8,128)S(1)} %fusion.21, s32[]{:T(128)} %constant.37.clone.1, s32[]{:T(128)} %constant.37.clone.1, s32[]{:T(128)S(6)} %select_n.146, s32[]{:T(128)S(6)} %select_n.147) | dynamic-update-slice | bytes 1048580 | tf_op jit(solution)/shard_map/dynamic_update_slice | solution.py:143
  185.9 1.9 slice.192
  187.8 1.9 collective-permute-start.7
  189.7 44.7 %collective-permute-done.7 = f32[1,2,256,1024]{2,3,1,0:T(8,128)S(1)} collective-permute-done((f32[1,2,256,1024]{2,3,1,0:T(8,128)S(1)}, f32[1,2,256,1024]{2,3,1,0:T(8,128)S(1)}, u32[]{:S(2)}, u32[]{:S(2)}) %collective-permute-start.7) | collective-permute-done | bytes 2097184 | tf_op jit(solution)/shard_map/ppermute | solution.py:11
  234.4 0.4 slice_add_fusion
  234.8 1.8 copy.23
  (51 shorter events, 2.1 us)
Async XLA Ops:
  0.0 37.1 %collective-permute-start = (f32[1,2,256,1024]{3,2,1,0:T(8,128)}, f32[1,2,256,1024]{3,2,1,0:T(8,128)S(1)}, u32[]{:S(2)}, u32[]{:S(2)}) collective-permute-start(f32[1,2,256,1024]{3,2,1,0:T(8,128)} %param.7), channel_id=1, source_target_pairs={{0,127},{1,0},{2,1},{3,2},{4,3},{5,4},{6,5},{7,6},{8,7},{9,8},{10,... | collective-permute-start | bytes 6291464 | tf_op jit(solution)/shard_map/ppermute | solution.py:11
  26.9 4.5 %copy-start.11 = (f32[1,2,256,1024]{3,2,1,0:T(8,128)S(1)}, f32[1,2,256,1024]{3,2,1,0:T(8,128)}, u32[]{:S(2)}) copy-start(f32[1,2,256,1024]{3,2,1,0:T(8,128)} %param.7) | copy-start | bytes 6291460
  40.2 20.3 %collective-permute-start.1 = (f32[2,2,256,256]{2,3,0,1:T(8,128)}, f32[2,2,256,256]{2,3,0,1:T(8,128)S(1)}, u32[]{:S(2)}, u32[]{:S(2)}) collective-permute-start(f32[2,2,256,256]{2,3,0,1:T(8,128)} %convolution_bitcast_fusion.14), channel_id=1, source_target_pairs={{0,128},{128,256},{256,384},{1,129},{129,257},{257,385},{2,130},{1... | collective-permute-start | bytes 3145736 | tf_op jit(solution)/shard_map/ppermute | solution.py:17
  60.4 1.0 copy-start.2
  63.4 27.0 %copy-start.16 = (bf16[2,256,256]{2,1,0:T(8,128)(2,1)S(1)}, bf16[2,256,256]{2,1,0:T(8,128)(2,1)}, u32[]{:S(2)}) copy-start(bf16[2,256,256]{2,1,0:T(8,128)(2,1)} %param.10) | copy-start | bytes 786436
  63.4 20.5 %collective-permute-start.2 = (f32[2,2,256,256]{2,3,0,1:T(8,128)}, f32[2,2,256,256]{2,3,0,1:T(8,128)S(1)}, u32[]{:S(2)}, u32[]{:S(2)}) collective-permute-start(f32[2,2,256,256]{2,3,0,1:T(8,128)} %convolution_bitcast_fusion.12), channel_id=1, source_target_pairs={{0,128},{128,256},{256,384},{1,129},{129,257},{257,385},{2,130},{1... | collective-permute-start | bytes 3145736 | tf_op jit(solution)/shard_map/ppermute | solution.py:17
  83.9 1.0 copy-start.4
  86.8 16.9 %collective-permute-start.3 = (f32[2,2,256,256]{2,3,0,1:T(8,128)}, f32[2,2,256,256]{2,3,0,1:T(8,128)S(1)}, u32[]{:S(2)}, u32[]{:S(2)}) collective-permute-start(f32[2,2,256,256]{2,3,0,1:T(8,128)} %convolution_bitcast_fusion.10), channel_id=1, source_target_pairs={{0,128},{128,256},{256,384},{1,129},{129,257},{257,385},{2,130},{1... | collective-permute-start | bytes 3145736 | tf_op jit(solution)/shard_map/ppermute | solution.py:17
  93.4 17.9 %copy-start.13 = (bf16[2,256,2,256,1]{3,1,2,0,4:T(8,128)(2,1)}, bf16[2,256,2,256,1]{3,1,2,0,4:T(8,128)(2,1)S(1)}, u32[]{:S(2)}) copy-start(bf16[2,256,2,256,1]{3,1,2,0,4:T(8,128)(2,1)S(1)} %fusion.126) | copy-start | bytes 1572868
  103.7 1.6 copy-start.6
  107.9 2.4 %copy-start.14 = (bf16[1,256,2,256]{3,1,2,0:T(8,128)(2,1)S(1)}, bf16[1,256,2,256]{3,1,2,0:T(8,128)(2,1)}, u32[]{:S(2)}) copy-start(bf16[1,256,2,256]{3,1,2,0:T(8,128)(2,1)} %get-tuple-element.37) | copy-start | bytes 786436
  107.9 2.4 %copy-start.15 = (bf16[1,256,2,256]{3,1,2,0:T(8,128)(2,1)S(1)}, bf16[1,256,2,256]{3,1,2,0:T(8,128)(2,1)}, u32[]{:S(2)}) copy-start(bf16[1,256,2,256]{3,1,2,0:T(8,128)(2,1)} %get-tuple-element.38) | copy-start | bytes 786436
  112.3 21.2 %copy-start.12 = (bf16[2,256,256]{2,1,0:T(8,128)(2,1)S(1)}, bf16[2,256,256]{2,1,0:T(8,128)(2,1)}, u32[]{:S(2)}) copy-start(bf16[2,256,256]{2,1,0:T(8,128)(2,1)} %param.8) | copy-start | bytes 786436
  112.3 16.1 %collective-permute-start.4 = (bf16[2,2,256,256]{2,3,0,1:T(8,128)(2,1)S(1)}, bf16[2,2,256,256]{2,3,0,1:T(8,128)(2,1)}, u32[]{:S(2)}, u32[]{:S(2)}) collective-permute-start(bf16[2,2,256,256]{2,3,0,1:T(8,128)(2,1)S(1)} %pad_maximum_fusion.2), channel_id=1, source_target_pairs={{128,0},{256,128},{384,256},{129,1},{257,129},{385,257},{130,2},{2... | collective-permute-start | bytes 1572872 | tf_op jit(solution)/shard_map/ppermute | solution.py:17
  131.6 16.1 %collective-permute-start.5 = (bf16[2,2,256,256]{2,3,0,1:T(8,128)(2,1)}, bf16[2,2,256,256]{2,3,0,1:T(8,128)(2,1)}, u32[]{:S(2)}, u32[]{:S(2)}) collective-permute-start(bf16[2,2,256,256]{2,3,0,1:T(8,128)(2,1)} %pad_maximum_fusion.3), channel_id=1, source_target_pairs={{128,0},{256,128},{384,256},{129,1},{257,129},{385,257},{130,2},{2... | collective-permute-start | bytes 1572872 | tf_op jit(solution)/shard_map/ppermute | solution.py:17
  150.8 3.7 %copy-start.3 = (f32[2,2,256,256]{2,3,0,1:T(8,128)S(1)}, f32[2,2,256,256]{2,3,0,1:T(8,128)}, u32[]{:S(2)}) copy-start(f32[2,2,256,256]{2,3,0,1:T(8,128)} %copy-done.2) | copy-start | bytes 3145732
  150.8 3.7 %copy-start.5 = (f32[2,2,256,256]{2,3,0,1:T(8,128)S(1)}, f32[2,2,256,256]{2,3,0,1:T(8,128)}, u32[]{:S(2)}) copy-start(f32[2,2,256,256]{2,3,0,1:T(8,128)} %copy-done.4) | copy-start | bytes 3145732
  150.8 5.1 %copy-start.1 = (f32[2,2,256,256]{2,3,0,1:T(8,128)S(1)}, f32[2,2,256,256]{2,3,0,1:T(8,128)}, u32[]{:S(2)}) copy-start(f32[2,2,256,256]{2,3,0,1:T(8,128)} %convolution_bitcast_fusion.5) | copy-start | bytes 3145732
  152.4 11.2 %collective-permute-start.6 = (bf16[2,2,256,256]{2,3,0,1:T(8,128)(2,1)S(1)}, bf16[2,2,256,256]{2,3,0,1:T(8,128)(2,1)}, u32[]{:S(2)}, u32[]{:S(2)}) collective-permute-start(bf16[2,2,256,256]{2,3,0,1:T(8,128)(2,1)S(1)} %pad_maximum_fusion.4), channel_id=1, source_target_pairs={{128,0},{256,128},{384,256},{129,1},{257,129},{385,257},{130,2},{2... | collective-permute-start | bytes 1572872 | tf_op jit(solution)/shard_map/ppermute | solution.py:17
  157.6 10.7 %copy-start.7 = (f32[1,2,1,256,256]{3,4,1,2,0:T(8,128)S(1)}, f32[1,2,1,256,256]{3,4,1,2,0:T(8,128)}, u32[]{:S(2)}) copy-start(f32[1,2,1,256,256]{3,4,1,2,0:T(8,128)} %get-tuple-element.7) | copy-start | bytes 1572868
  157.6 10.7 %copy-start.8 = (f32[1,2,1,256,256]{3,4,1,2,0:T(8,128)S(1)}, f32[1,2,1,256,256]{3,4,1,2,0:T(8,128)}, u32[]{:S(2)}) copy-start(f32[1,2,1,256,256]{3,4,1,2,0:T(8,128)} %get-tuple-element.8) | copy-start | bytes 1572868
  166.7 1.6 copy-start.9
  166.7 1.6 copy-start.10
  185.9 48.5 %copy-start = (f32[1,2,512,1024]{2,3,1,0:T(8,128)S(1)}, f32[1,2,512,1024]{2,3,1,0:T(8,128)}, u32[]{:S(2)}) copy-start(f32[1,2,512,1024]{2,3,1,0:T(8,128)} %dynamic_update_slice.7) | copy-start | bytes 12582916
  187.8 46.6 %collective-permute-start.7 = (f32[1,2,256,1024]{2,3,1,0:T(8,128)S(1)}, f32[1,2,256,1024]{2,3,1,0:T(8,128)S(1)}, u32[]{:S(2)}, u32[]{:S(2)}) collective-permute-start(f32[1,2,256,1024]{2,3,1,0:T(8,128)S(1)} %slice.192), channel_id=1, source_target_pairs={{0,1},{1,2},{2,3},{3,4},{4,5},{5,6},{6,7},{7,8},{8,9},{9,10},{10,1... | collective-permute-start | bytes 6291464 | tf_op jit(solution)/shard_map/ppermute | solution.py:11
where the time goes:
time: 238 us; the launch traced here: 237 us
  waiting for transfers between devices  125 us (53%)
  starting transfers between devices  31.7 us (13%)
  local copies, waits for them, and re-layouts  30.8 us (13%)
  matrix products  25.2 us (11%)
  other arithmetic  15.3 us (6%)
  between operations  8.65 us (4%)
    ppermute x6, waiting for transfers between devices, shifted_2(): lax.ppermute(value, axis, [(source, source + steps) for source in range(f...  74.8 us
    ppermute x2, waiting for transfers between devices, shifted(): lax.ppermute(shard, axis, [(i, (i + by) % size) for i in range(size)])  50.2 us
    ppermute x6, starting transfers between devices, shifted_2(): lax.ppermute(value, axis, [(source, source + steps) for source in range(f...  16.4 us
    ppermute x2, starting transfers between devices, shifted(): lax.ppermute(shard, axis, [(i, (i + by) % size) for i in range(size)])  15.2 us
    dynamic_update_slice x2, local copies, waits for them, and re-layouts, scatter_windows(): lax.dynamic_update_slice(frame, current + gradients[:, view_index], corner)  13.3 us
    dot_general x5, matrix products, back_left(): jnp.einsum('dicj,vdix->vcjx', matrix, gradient, preferred_element_type=jn...  9.58 us
    dot_general x5, matrix products, apply_right(): jnp.einsum('vcyj,dicj->vdyi', wavefield, matrix, preferred_element_type=j...  7.79 us
  transfers between devices with their start and end apart: 8, of which 8 were waited for; matrix products, arithmetic and copies ran while one was open for 8% of the time, Pallas kernels for 0%

commit v1 on v0

v1 whole, which is shorter than its diff:
```python
import functools
import math

import jax
import jax.numpy as jnp
import numpy as np
from jax import lax
from jax.experimental import pallas as pl
from jax.experimental.pallas import tpu as pltpu
from jax.sharding import PartitionSpec as P

MESH = pl.DeviceIdType.MESH
BF = jnp.bfloat16
F32 = jnp.float32
SIDE = 256
CHUNKS = 4
ROWS = SIDE // CHUNKS
BLOCKS = 4


def fourier_constants():
    index = np.arange(SIDE)
    angle = 2.0 * math.pi * ((index[:, None] * index[None, :]) % SIDE) / SIDE
    return np.stack([np.cos(angle) / 16.0, -np.sin(angle) / 16.0]).astype(np.float32)


def mm(a, b):
    return jnp.dot(a, b, preferred_element_type=F32)


def block(real, imag):
    upper = jnp.concatenate([real, -imag], axis=1)
    lower = jnp.concatenate([imag, real], axis=1)
    return jnp.concatenate([upper, lower], axis=0)


def block_t(real, imag):
    upper = jnp.concatenate([real, imag], axis=1)
    lower = jnp.concatenate([-imag, real], axis=1)
    return jnp.concatenate([upper, lower], axis=0)


def wide(row):
    return jnp.concatenate([row, row], axis=1)


def each(count, action):
    def step(i, carry):
        action(i)
        return carry

    lax.fori_loop(0, count, step, 0)


def column_select(obj, part, chunk, start):
    lane = lax.broadcasted_iota(jnp.int32, (1, SIDE), 1)
    rows = pl.ds(pl.multiple_of(chunk * ROWS, ROWS), ROWS)
    picked = jnp.zeros((ROWS, SIDE), F32)
    for b in range(BLOCKS):
        column = lane + b * SIDE
        inside = (column >= start) & (column < start + SIDE)
        picked = jnp.where(inside, obj[part, rows, b * SIDE:(b + 1) * SIDE], picked)
    return picked


def row_index(chunk):
    return lax.broadcasted_iota(jnp.int32, (ROWS, SIDE), 0) + chunk * ROWS


def to_lanes(value):
    low = value.astype(BF)
    return jnp.concatenate([low[:SIDE], low[SIDE:]], axis=1)


def to_rows(value):
    low = value.astype(BF)
    return jnp.concatenate([low[:, :SIDE], low[:, SIDE:]], axis=0)


def wave_kernel(
    n_tile,
    obj_in, probe_in, chirp_in, amp_in, srow_in, scol_in, count, tab_in,
    out,
    obj, probe, chirp, amp, srow, scol, tab,
    pos, send_a, recv_a, send_b, recv_b, asm, win, grad, got, total,
    first, second, psi, vert, residual,
    in_sem, obj_sem, pos_sem, amp_sem, a_sem, b_sem, xs_sem, xr_sem, gs_sem, gr_sem, fs_sem, fr_sem,
    out_sem,
):
    k = lax.axis_index("cuts")
    t = lax.axis_index("tile")
    core = lax.rem(t, 2)
    following = lax.rem(t + 1, n_tile)
    previous = lax.rem(t + n_tile - 1, n_tile)
    alpha = k // 2
    computing = lax.rem(k, 2) == core

    def target(which):
        return 2 * which + core

    ints = [
        pltpu.make_async_copy(srow_in, srow, in_sem.at[0]),
        pltpu.make_async_copy(scol_in, scol, in_sem.at[1]),
    ]
    tables = [
        pltpu.make_async_copy(chirp_in, chirp, in_sem.at[3]),
        pltpu.make_async_copy(tab_in, tab, in_sem.at[4]),
        pltpu.make_async_copy(probe_in, probe, in_sem.at[5]),
        pltpu.make_async_copy(amp_in.at[0], amp.at[0], in_sem.at[6]),
    ]

    def load(c):
        rows = pl.ds(pl.multiple_of(c * ROWS, ROWS), ROWS)
        return pltpu.make_async_copy(obj_in.at[0, :, rows], obj.at[:, rows], obj_sem.at[c])

    barrier = pltpu.get_barrier_semaphore()
    for step in range(1, 4):
        pl.semaphore_signal(
            barrier, inc=1, device_id=(lax.rem(k + step, 4), t), device_id_type=MESH
        )
    for neighbour in (following, previous):
        pl.semaphore_signal(barrier, inc=1, device_id=(k, neighbour), device_id_type=MESH)

    for copy in ints:
        copy.start()
    each(CHUNKS, lambda c: load(c).start())

    @pl.when(computing)
    def _():
        for copy in tables:
            copy.start()

    for copy in ints:
        copy.wait()
    line = lax.broadcasted_iota(jnp.int32, (8, 128), 0)
    mine = jnp.zeros((8, 128), jnp.int32)
    for i, value in enumerate((srow[0], srow[1], scol[0], scol[1], count[0])):
        mine = jnp.where(line == i, value, mine)
    pos[0] = mine
    pl.semaphore_wait(barrier, 5)

    def remote(source, sink, send, recv, device):
        return pltpu.make_async_remote_copy(
            src_ref=source, dst_ref=sink, send_sem=send, recv_sem=recv,
            device_id=device, device_id_type=MESH,
        )

    pos_copy = remote(pos.at[0], pos.at[1], pos_sem.at[0], pos_sem.at[1], (k, following))
    pos_copy.start()

    def a_copy(c):
        return remote(send_a.at[c], recv_a.at[c], a_sem.at[0, c], a_sem.at[1, c], (k, following))

    def b_copy(c):
        return remote(send_b.at[c], recv_b.at[c], b_sem.at[0, c], b_sem.at[1, c], (k, previous))

    start_a = wide(pos[0, 3:4, :])

    def begin_a(c):
        load(c).wait()
        for part in range(2):
            send_a[c, part] = column_select(obj, part, c, start_a).astype(BF)
        a_copy(c).start()

    each(CHUNKS, begin_a)

    amp_copy = remote(amp_in.at[1], amp.at[1], amp_sem.at[0], amp_sem.at[1], (k, following))
    sends_amp = (alpha == 1) & (lax.rem(k, 2) == lax.rem(following, 2))
    takes_amp = (alpha == 1) & computing

    @pl.when(sends_amp)
    def _():
        amp_copy.start()

    @pl.when(computing)
    def _():
        for copy in tables:
            copy.wait()
        t_r, t_i = tab[0].astype(BF), tab[1].astype(BF)
        first[1] = block(t_r, t_i)
        second[1] = block_t(t_r, t_i)
        angle = chirp[...]
        turn_r, turn_i = jnp.cos(angle), jnp.sin(angle)
        s_r = tab[0] * turn_r + tab[1] * turn_i
        s_i = tab[0] * turn_i - tab[1] * turn_r
        scaled = jnp.concatenate([s_r, s_i], axis=1)
        big = scaled.astype(BF)
        small = (scaled - big.astype(F32)).astype(BF)
        f_high = second[1]
        f_low = block_t((tab[0] - t_r.astype(F32)).astype(BF), (tab[1] - t_i.astype(F32)).astype(BF))
        prop = mm(big, f_high) + (mm(big, f_low) + mm(small, f_high))
        p_r, p_i = prop[:, :SIDE], prop[:, SIDE:]
        first[0] = block(p_r.astype(BF), p_i.astype(BF))
        second[0] = block_t(p_r.T.astype(BF), p_i.T.astype(BF))

    pos_copy.wait_recv()
    start_b = wide(pos[1, 2:3, :])

    def begin_b(c):
        for part in range(2):
            send_b[c, part] = column_select(obj, part, c, start_b).astype(BF)
        b_copy(c).start()

    each(CHUNKS, begin_b)

    @pl.when(computing)
    def _():
        first_slot = alpha == 0
        row_start = wide(jnp.where(first_slot, pos[0, 0:1, :], pos[1, 1:2, :]))
        col_start = wide(jnp.where(first_slot, pos[0, 2:3, :], pos[1, 3:4, :]))
        down = lax.broadcasted_iota(jnp.int32, (SIDE, SIDE), 0)
        across = lax.broadcasted_iota(jnp.int32, (SIDE, SIDE), 1)
        row_turn = jnp.where(((down - across - row_start) & (SIDE - 1)) == 0, 1.0, 0.0).astype(BF)
        col_turn = jnp.where(((across - down - col_start) & (SIDE - 1)) == 0, 1.0, 0.0).astype(BF)
        for part in range(2):
            half = mm(row_turn, probe[part]).astype(BF)
            psi[0, :, part * SIDE:(part + 1) * SIDE] = mm(half, col_turn)

    def send_window(which, c):
        return remote(
            asm.at[which, c], win.at[k, c], xs_sem.at[which, c], xr_sem.at[k, c],
            (target(which), t),
        )

    edge = [wide(pos[0, 0:1, :]), wide(pos[1, 1:2, :])]
    left = [wide(pos[0, 2:3, :]), wide(pos[1, 3:4, :])]

    def put_together(which, c):
        own = [column_select(obj, part, c, left[which]) for part in range(2)]
        upper = row_index(c) >= edge[which]
        if which == 1:
            a_copy(c).wait_recv()
        else:
            b_copy(c).wait_recv()
        for part in range(2):
            if which == 1:
                piece = jnp.where(upper, recv_a[c, part].astype(F32), own[part])
            else:
                piece = jnp.where(upper, own[part], recv_b[c, part].astype(F32))
            asm[which, c, part] = piece.astype(BF)

        @pl.when(k != target(which))
        def _():
            send_window(which, c).start()

        @pl.when(k == target(which))
        def _():
            win[k, c] = asm[which, c]

    each(CHUNKS, lambda c: put_together(1, c))
    each(CHUNKS, lambda c: put_together(0, c))

    def give_back(layer, c):
        return remote(
            grad.at[layer, c], got.at[alpha, c], gs_sem.at[layer, c], gr_sem.at[alpha, c],
            (layer, t),
        )

    def give_whole(layer):
        return remote(
            grad.at[layer], got.at[alpha], gs_sem.at[layer, 0], gr_sem.at[alpha, 0], (layer, t)
        )

    @pl.when(computing)
    def _():
        def window(layer):
            return [win[layer, :, part].reshape(SIDE, SIDE).astype(F32) for part in range(2)]

        def ahead(layer):
            @pl.when(k != layer)
            def _():
                each(CHUNKS, lambda c: remote(
                    win.at[layer, c], win.at[layer, c], xs_sem.at[0, c], xr_sem.at[layer, c], (layer, t)
                ).wait_recv())

            far = layer // 3
            w_r, w_i = window(layer)
            s_r, s_i = psi[layer, :, :SIDE], psi[layer, :, SIDE:]
            vert[:SIDE] = (s_r * w_r - s_i * w_i).astype(BF)
            vert[SIDE:] = (s_r * w_i + s_i * w_r).astype(BF)
            psi[layer + 1] = mm(to_lanes(mm(first[far], vert[...])), second[far])

        each(4, ahead)

        e_r, e_i = psi[4, :, :SIDE], psi[4, :, SIDE:]

        @pl.when(takes_amp)
        def _():
            amp_copy.wait_recv()

        live = wide(
            jnp.where(
                alpha == 0, jnp.where(pos[0, 4:5, :] > 0, 1.0, 0.0), jnp.where(pos[1, 4:5, :] > 1, 1.0, 0.0)
            )
        )
        measured = amp[alpha].astype(F32)
        factor = live * (1.0 - measured * lax.rsqrt(e_r * e_r + e_i * e_i + 0.01))
        residual[:, :SIDE] = (factor * e_r).astype(BF)
        residual[:, SIDE:] = (factor * e_i).astype(BF)

        def behind(step):
            layer = 3 - step
            far = layer // 3
            back = mm(second[far], to_rows(mm(residual[...], first[far])))
            h_r, h_i = back[:SIDE], back[SIDE:]
            s_r, s_i = psi[layer, :, :SIDE], psi[layer, :, SIDE:]
            w_r, w_i = window(layer)
            grad[layer, :, 0] = (h_r * s_r + h_i * s_i).astype(BF).reshape(CHUNKS, ROWS, SIDE)
            grad[layer, :, 1] = (h_i * s_r - h_r * s_i).astype(BF).reshape(CHUNKS, ROWS, SIDE)
            residual[:, :SIDE] = (h_r * w_r + h_i * w_i).astype(BF)
            residual[:, SIDE:] = (h_i * w_r - h_r * w_i).astype(BF)

            @pl.when((k != layer) & (layer > 0))
            def _():
                give_whole(layer).start()

            @pl.when((k != layer) & (layer == 0))
            def _():
                each(CHUNKS, lambda c: give_back(layer, c).start())

            @pl.when(k == layer)
            def _():
                got[alpha] = grad[layer]

        each(4, behind)

    def forward(which, c):
        return remote(
            got.at[which, c], got.at[2 + which, c], fs_sem.at[which, c], fr_sem.at[which, c],
            (k, following if which == 0 else previous),
        )

    for which in (1, 0):
        @pl.when((k != target(which)) & (k > 0))
        def _():
            remote(
                grad.at[0], got.at[which], gs_sem.at[0, 0], gr_sem.at[which, 0], (target(which), t)
            ).wait_recv()

        def collect(c):
            @pl.when((k != target(which)) & (k == 0))
            def _():
                remote(
                    grad.at[0, c], got.at[which, c], gs_sem.at[0, c], gr_sem.at[which, c], (target(which), t)
                ).wait_recv()

            forward(which, c).start()

        each(CHUNKS, collect)

    def give_out(c):
        rows = pl.ds(pl.multiple_of(c * ROWS, ROWS), ROWS)
        return pltpu.make_async_copy(total.at[:, rows], out.at[0, :, rows], out_sem.at[c])

    edges = [edge[0], edge[1], wide(pos[1, 0:1, :]), wide(pos[0, 1:2, :])]
    lefts = [left[0], left[1], wide(pos[1, 2:3, :]), wide(pos[0, 3:4, :])]
    lane = lax.broadcasted_iota(jnp.int32, (1, SIDE), 1)

    def add_up(c):
        rows = pl.ds(pl.multiple_of(c * ROWS, ROWS), ROWS)
        row = row_index(c)
        for which in range(2):
            forward(which, c).wait_recv()
        for part in range(2):
            pieces = []
            for s in range(4):
                held = row >= edges[s] if s in (0, 3) else row < edges[s]
                pieces.append(jnp.where(held, got[s, c, part].astype(F32), 0.0))
            for b in range(BLOCKS):
                column = lane + b * SIDE
                sums = jnp.zeros((ROWS, SIDE), F32)
                for s in range(4):
                    inside = (column >= lefts[s]) & (column < lefts[s] + SIDE)
                    sums = sums + jnp.where(inside, pieces[s], 0.0)
                total[part, rows, b * SIDE:(b + 1) * SIDE] = sums
        give_out(c).start()

    each(CHUNKS, add_up)

    pos_copy.wait_send()

    @pl.when(sends_amp)
    def _():
        amp_copy.wait_send()

    def finish(c):
        a_copy(c).wait_send()
        b_copy(c).wait_send()
        for which in range(2):
            @pl.when(k != target(which))
            def _():
                send_window(which, c).wait_send()

    each(CHUNKS, finish)

    @pl.when(computing)
    def _():
        def given(layer):
            @pl.when((k != layer) & (layer > 0))
            def _():
                give_whole(layer).wait_send()

            @pl.when((k != layer) & (layer == 0))
            def _():
                each(CHUNKS, lambda c: give_back(layer, c).wait_send())

        each(4, given)

    def leave(c):
        for which in range(2):
            forward(which, c).wait_send()
        give_out(c).wait()

    each(CHUNKS, leave)


def body(object_field, probe_wave, chirp_phase, amplitude, scan_row, scan_col, view_count):
    n_tile = lax.axis_size("tile")
    anywhere = pl.BlockSpec(memory_space=pl.ANY)
    dma = pltpu.SemaphoreType.DMA
    return pl.pallas_call(
        functools.partial(wave_kernel, n_tile),
        out_shape=pltpu.VMEM((1, 2, SIDE, BLOCKS * SIDE), F32),
        in_specs=[anywhere] * 6 + [pl.BlockSpec(memory_space=pltpu.SMEM), anywhere],
        out_specs=anywhere,
        scratch_shapes=[
            pltpu.VMEM((2, SIDE, BLOCKS * SIDE), F32),
            pltpu.VMEM((2, SIDE, SIDE), BF),
            pltpu.VMEM((1, SIDE), F32),
            pltpu.VMEM((2, SIDE, SIDE), BF),
            pltpu.SMEM((2,), jnp.int32),
            pltpu.SMEM((2,), jnp.int32),
            pltpu.VMEM((2, SIDE, SIDE), F32),
            pltpu.VMEM((2, 8, 128), jnp.int32),
            pltpu.VMEM((CHUNKS, 2, ROWS, SIDE), BF),
            pltpu.VMEM((CHUNKS, 2, ROWS, SIDE), BF),
            pltpu.VMEM((CHUNKS, 2, ROWS, SIDE), BF),
            pltpu.VMEM((CHUNKS, 2, ROWS, SIDE), BF),
            pltpu.VMEM((2, CHUNKS, 2, ROWS, SIDE), BF),
            pltpu.VMEM((4, CHUNKS, 2, ROWS, SIDE), BF),
            pltpu.VMEM((4, CHUNKS, 2, ROWS, SIDE), BF),
            pltpu.VMEM((4, CHUNKS, 2, ROWS, SIDE), BF),
            pltpu.VMEM((2, SIDE, BLOCKS * SIDE), F32),
            pltpu.VMEM((2, 2 * SIDE, 2 * SIDE), BF),
            pltpu.VMEM((2, 2 * SIDE, 2 * SIDE), BF),
            pltpu.VMEM((5, SIDE, 2 * SIDE), F32),
            pltpu.VMEM((2 * SIDE, SIDE), BF),
            pltpu.VMEM((SIDE, 2 * SIDE), BF),
            dma((7,)),
            dma((CHUNKS,)),
            dma((2,)),
            dma((2,)),
            dma((2, CHUNKS)),
            dma((2, CHUNKS)),
            dma((2, CHUNKS)),
            dma((4, CHUNKS)),
            dma((4, CHUNKS)),
            dma((2, CHUNKS)),
            dma((2, CHUNKS)),
            dma((2, CHUNKS)),
            dma((CHUNKS,)),
        ],
        compiler_params=pltpu.CompilerParams(
            collective_id=0, has_side_effects=True, vmem_limit_bytes=48 * 1024 * 1024
        ),
        name="waves",
    )(
        *(
            value if value.size == 1 else pltpu.with_memory_space_constraint(value, pltpu.HBM)
            for value in (
                object_field, probe_wave, chirp_phase.reshape(1, SIDE), amplitude,
                scan_row, scan_col, view_count, jnp.asarray(fourier_constants()),
            )
        )
    )


def solution(mesh):
    in_specs = (
        P("cuts", None, "tile", None),
        P(),
        P(),
        P("tile", None, None),
        P("tile"),
        P("tile"),
        P("tile"),
    )
    return jax.shard_map(
        body, mesh=mesh, in_specs=in_specs, out_specs=P("cuts", None, "tile", None), check_vma=False
    )
```

time: 238 us -> 45.2 us (0.19)
  the two profiles are of different devices: /device:TPU:2 before, /device:TPU:4 now
where the time goes in v1:
time: 45.2 us; the launch traced here: 45.1 us
  Pallas kernels  43.1 us (95%)
  local copies, waits for them, and re-layouts  1.32 us (3%)
  between operations  0.66 us (1%)
    pallas_call x1, Pallas kernels, body(): pl.pallas_call(functools.partial(wave_kernel, n_tile), out_shape=pltpu.VM...  43.1 us
    unnamed x1, local copies, waits for them, and re-layouts  1.32 us

profile of v1, /device:TPU:4, one launch (start us, length us, event | category | flops | bytes accessed | tf_op | source)
XLA Modules:
  0.0 45.1 jit_solution(7173108304023658730)
XLA Ops:
  0.7 43.1 %waves.1 = f32[1,2,256,1024]{3,2,1,0:T(8,128)S(1)} custom-call(f32[1,2,256,1024]{3,2,1,0:T(8,128)} %obj_in.1, bf16[2,256,256]{2,1,0:T(8,128)(2,1)} %probe_in.1, f32[1,256]{1,0:T(1,128)} %bitcast.1, bf16[2,256,256]{2,1,0:T(8,128)(2,1)} %amp_in.1, s32[2]{0:T(128)} %srow_in.1, s32[2]{0:T(128)} %scol_in.1, s32[1]{0:T(128)S(6)} %copy.11.count, ...), custom_call_target="tpu_custom_call" | custom-call | tf_op jit(solution)/shard_map/waves/pallas_call | solution.py:421
  43.8 1.3 %copy.10 = f32[1,2,256,1024]{3,2,1,0:T(8,128)} copy(f32[1,2,256,1024]{3,2,1,0:T(8,128)S(1)} %waves.1) | data formatting | bytes 4194304

commit v2 on v1

--- a/solution.py
+++ b/solution.py
@@ -65,16 +65,6 @@
 
 def row_index(chunk):
     return lax.broadcasted_iota(jnp.int32, (ROWS, SIDE), 0) + chunk * ROWS
-
-
-def to_lanes(value):
-    low = value.astype(BF)
-    return jnp.concatenate([low[:SIDE], low[SIDE:]], axis=1)
-
-
-def to_rows(value):
-    low = value.astype(BF)
-    return jnp.concatenate([low[:, :SIDE], low[:, SIDE:]], axis=0)
 
 
 def wave_kernel(
@@ -247,18 +237,19 @@
         def _():
             win[k, c] = asm[which, c]
 
-    each(CHUNKS, lambda c: put_together(1, c))
-    each(CHUNKS, lambda c: put_together(0, c))
+    def near_first(action):
+        for side, order in ((0, (0, 1)), (1, (1, 0))):
+            @pl.when(core == side)
+            def _():
+                for which in order:
+                    each(CHUNKS, functools.partial(action, which))
+
+    near_first(put_together)
 
     def give_back(layer, c):
         return remote(
             grad.at[layer, c], got.at[alpha, c], gs_sem.at[layer, c], gr_sem.at[alpha, c],
             (layer, t),
-        )
-
-    def give_whole(layer):
-        return remote(
-            grad.at[layer], got.at[alpha], gs_sem.at[layer, 0], gr_sem.at[alpha, 0], (layer, t)
         )
 
     @pl.when(computing)
@@ -278,7 +269,12 @@
             s_r, s_i = psi[layer, :, :SIDE], psi[layer, :, SIDE:]
             vert[:SIDE] = (s_r * w_r - s_i * w_i).astype(BF)
             vert[SIDE:] = (s_r * w_i + s_i * w_r).astype(BF)
-            psi[layer + 1] = mm(to_lanes(mm(first[far], vert[...])), second[far])
+            for part in range(2):
+                side = slice(part * SIDE, (part + 1) * SIDE)
+                residual[:, side] = mm(first[far, side], vert[...]).astype(BF)
+            for part in range(2):
+                side = slice(part * SIDE, (part + 1) * SIDE)
+                psi[layer + 1, :, side] = mm(residual[...], second[far, :, side])
 
         each(4, ahead)
 
@@ -301,8 +297,10 @@
         def behind(step):
             layer = 3 - step
             far = layer // 3
-            back = mm(second[far], to_rows(mm(residual[...], first[far])))
-            h_r, h_i = back[:SIDE], back[SIDE:]
+            for part in range(2):
+                side = slice(part * SIDE, (part + 1) * SIDE)
+                vert[side] = mm(residual[...], first[far, :, side]).astype(BF)
+            h_r, h_i = mm(second[far, :SIDE], vert[...]), mm(second[far, SIDE:], vert[...])
             s_r, s_i = psi[layer, :, :SIDE], psi[layer, :, SIDE:]
             w_r, w_i = window(layer)
             grad[layer, :, 0] = (h_r * s_r + h_i * s_i).astype(BF).reshape(CHUNKS, ROWS, SIDE)
@@ -310,11 +308,7 @@
             residual[:, :SIDE] = (h_r * w_r + h_i * w_i).astype(BF)
             residual[:, SIDE:] = (h_i * w_r - h_r * w_i).astype(BF)
 
-            @pl.when((k != layer) & (layer > 0))
-            def _():
-                give_whole(layer).start()
-
-            @pl.when((k != layer) & (layer == 0))
+            @pl.when(k != layer)
             def _():
                 each(CHUNKS, lambda c: give_back(layer, c).start())
 
@@ -330,23 +324,16 @@
             (k, following if which == 0 else previous),
         )
 
-    for which in (1, 0):
-        @pl.when((k != target(which)) & (k > 0))
+    def collect(which, c):
+        @pl.when(k != target(which))
         def _():
             remote(
-                grad.at[0], got.at[which], gs_sem.at[0, 0], gr_sem.at[which, 0], (target(which), t)
+                grad.at[0, c], got.at[which, c], gs_sem.at[0, c], gr_sem.at[which, c], (target(which), t)
             ).wait_recv()
 
-        def collect(c):
-            @pl.when((k != target(which)) & (k == 0))
-            def _():
-                remote(
-                    grad.at[0, c], got.at[which, c], gs_sem.at[0, c], gr_sem.at[which, c], (target(which), t)
-                ).wait_recv()
-
-            forward(which, c).start()
-
-        each(CHUNKS, collect)
+        forward(which, c).start()
+
+    near_first(collect)
 
     def give_out(c):
         rows = pl.ds(pl.multiple_of(c * ROWS, ROWS), ROWS)
@@ -396,11 +383,7 @@
     @pl.when(computing)
     def _():
         def given(layer):
-            @pl.when((k != layer) & (layer > 0))
-            def _():
-                give_whole(layer).wait_send()
-
-            @pl.when((k != layer) & (layer == 0))
+            @pl.when(k != layer)
             def _():
                 each(CHUNKS, lambda c: give_back(layer, c).wait_send())
 

time: 45.2 us -> 43.3 us (0.958)
  the two profiles are of different devices: /device:TPU:4 before, /device:TPU:2 now
where the time goes in v2:
time: 43.3 us; the launch traced here: 43.2 us
  Pallas kernels  41.2 us (95%)
  local copies, waits for them, and re-layouts  1.32 us (3%)
  between operations  0.66 us (2%)
    pallas_call x1, Pallas kernels, body(): pl.pallas_call(functools.partial(wave_kernel, n_tile), out_shape=pltpu.VM...  41.2 us
    unnamed x1, local copies, waits for them, and re-layouts  1.32 us

profile of v2, /device:TPU:2, one launch (start us, length us, event | category | flops | bytes accessed | tf_op | source)
XLA Modules:
  0.0 43.2 jit_solution(1453388960792360672)
XLA Ops:
  0.7 41.2 %waves.1 = f32[1,2,256,1024]{3,2,1,0:T(8,128)S(1)} custom-call(f32[1,2,256,1024]{3,2,1,0:T(8,128)} %obj_in.1, bf16[2,256,256]{2,1,0:T(8,128)(2,1)} %probe_in.1, f32[1,256]{1,0:T(1,128)} %bitcast.1, bf16[2,256,256]{2,1,0:T(8,128)(2,1)} %amp_in.1, s32[2]{0:T(128)} %srow_in.1, s32[2]{0:T(128)} %scol_in.1, s32[1]{0:T(128)S(6)} %copy.11.count, ...), custom_call_target="tpu_custom_call" | custom-call | tf_op jit(solution)/shard_map/waves/pallas_call | solution.py:404
  41.9 1.3 %copy.10 = f32[1,2,256,1024]{3,2,1,0:T(8,128)} copy(f32[1,2,256,1024]{3,2,1,0:T(8,128)S(1)} %waves.1) | data formatting | bytes 4194304

commit v3 on v2

--- a/solution.py
+++ b/solution.py
@@ -13,7 +13,7 @@
 BF = jnp.bfloat16
 F32 = jnp.float32
 SIDE = 256
-CHUNKS = 4
+CHUNKS = 8
 ROWS = SIDE // CHUNKS
 BLOCKS = 4
 

time: 43.3 us -> 44.1 us (1.018)
  Pallas kernels: 41.2 us -> 42 us
    pallas_call x1, Pallas kernels: 41.2 us -> 42 us  [body(): pl.pallas_call(functools.partial(wave_kernel, n_tile), out_shape=pltpu.VM...]
where the time goes in v3:
time: 44.1 us; the launch traced here: 44 us
  Pallas kernels  42 us (95%)
  local copies, waits for them, and re-layouts  1.32 us (3%)
  between operations  0.66 us (1%)
    pallas_call x1, Pallas kernels, body(): pl.pallas_call(functools.partial(wave_kernel, n_tile), out_shape=pltpu.VM...  42 us
    unnamed x1, local copies, waits for them, and re-layouts  1.32 us

profile of v3, /device:TPU:2, one launch (start us, length us, event | category | flops | bytes accessed | tf_op | source)
XLA Modules:
  0.0 44.0 jit_solution(17187302224191816127)
XLA Ops:
  0.7 42.0 %waves.1 = f32[1,2,256,1024]{3,2,1,0:T(8,128)S(1)} custom-call(f32[1,2,256,1024]{3,2,1,0:T(8,128)} %obj_in.1, bf16[2,256,256]{2,1,0:T(8,128)(2,1)} %probe_in.1, f32[1,256]{1,0:T(1,128)} %bitcast.1, bf16[2,256,256]{2,1,0:T(8,128)(2,1)} %amp_in.1, s32[2]{0:T(128)} %srow_in.1, s32[2]{0:T(128)} %scol_in.1, s32[1]{0:T(128)S(6)} %copy.11.count, ...), custom_call_target="tpu_custom_call" | custom-call | tf_op jit(solution)/shard_map/waves/pallas_call | solution.py:404
  42.7 1.3 %copy.10 = f32[1,2,256,1024]{3,2,1,0:T(8,128)} copy(f32[1,2,256,1024]{3,2,1,0:T(8,128)S(1)} %waves.1) | data formatting | bytes 4194304

commit v4 on v3

--- a/solution.py
+++ b/solution.py
@@ -13,7 +13,7 @@
 BF = jnp.bfloat16
 F32 = jnp.float32
 SIDE = 256
-CHUNKS = 8
+CHUNKS = 2
 ROWS = SIDE // CHUNKS
 BLOCKS = 4
 

time: 44.1 us -> 43.1 us (0.977)
  Pallas kernels: 42 us -> 41 us
    pallas_call x1, Pallas kernels: 42 us -> 41 us  [body(): pl.pallas_call(functools.partial(wave_kernel, n_tile), out_shape=pltpu.VM...]
where the time goes in v4:
time: 43.1 us; the launch traced here: 42.9 us
  Pallas kernels  41 us (95%)
  local copies, waits for them, and re-layouts  1.32 us (3%)
  between operations  0.66 us (2%)
    pallas_call x1, Pallas kernels, body(): pl.pallas_call(functools.partial(wave_kernel, n_tile), out_shape=pltpu.VM...  41 us
    unnamed x1, local copies, waits for them, and re-layouts  1.32 us

profile of v4, /device:TPU:2, one launch (start us, length us, event | category | flops | bytes accessed | tf_op | source)
XLA Modules:
  0.0 42.9 jit_solution(11059537632309548066)
XLA Ops:
  0.7 41.0 %waves.1 = f32[1,2,256,1024]{3,2,1,0:T(8,128)S(1)} custom-call(f32[1,2,256,1024]{3,2,1,0:T(8,128)} %obj_in.1, bf16[2,256,256]{2,1,0:T(8,128)(2,1)} %probe_in.1, f32[1,256]{1,0:T(1,128)} %bitcast.1, bf16[2,256,256]{2,1,0:T(8,128)(2,1)} %amp_in.1, s32[2]{0:T(128)} %srow_in.1, s32[2]{0:T(128)} %scol_in.1, s32[1]{0:T(128)S(6)} %copy.11.count, ...), custom_call_target="tpu_custom_call" | custom-call | tf_op jit(solution)/shard_map/waves/pallas_call | solution.py:404
  41.6 1.3 %copy.10 = f32[1,2,256,1024]{3,2,1,0:T(8,128)} copy(f32[1,2,256,1024]{3,2,1,0:T(8,128)S(1)} %waves.1) | data formatting | bytes 4194304
